TPU v7x, 32 devices: a whole 2x2x4 slice. The times are simulated.
32 devices in a mesh: groups: 2 (over y), row: 4 (over z), col: 2 (over x), src: 2 (over core).
Axes of the slice: x: 2, y: 2, z: 4, core: 2. Of those that a mesh axis runs over, the one named last changes fastest.
Arguments:
- impedance: bfloat16 [1024, 49152], P(('groups', 'row'), ('col', 'src')), parts along dimension 0, may hold values from -0.0390625 to 0.0390625
- currents: bfloat16 [16, 49152], P('groups', ('col', 'src', 'row')), parts along dimension 0, may hold values from -6 to 6
- tested: bfloat16 [16, 512], P('groups', ('row', 'col', 'src')), parts along dimension 0, may hold values from -6 to 6
Outputs:
- forward_field: float32 [16, 512], P('groups', ('row', 'col', 'src')), parts along dimension 0
- adjoint_field: float32 [16, 49152], P('groups', ('col', 'src', 'row')), parts along dimension 0
There are 2 independent parts, one for each index of `groups`. A program takes and returns all parts, laid end to end along the dimension named above; each array names one. Nothing has to cross between parts.
All inputs are finite; a program needn't handle non-finite values.
Results may differ from a plain program's by a relative error of at most 0.0003.
Values may be sent and summed in bfloat16 or wider, within the bound.
A program may use at most 64 MiB of HBM per device.

v0:
```python
import jax
import jax.numpy as jnp
from jax import lax
from jax.sharding import PartitionSpec as P


def body(impedance, currents, tested):
    col_block = lax.all_gather(currents, "row", axis=1, tiled=True)
    row_block = lax.all_gather(tested, ("col", "src"), axis=1, tiled=True)
    forward_terms = lax.dot_general(
        col_block, impedance, (((1,), (1,)), ((), ())), preferred_element_type=jnp.float32
    )
    adjoint_terms = jnp.dot(row_block, impedance, preferred_element_type=jnp.float32)
    forward_field = lax.psum_scatter(forward_terms, ("col", "src"), scatter_dimension=1, tiled=True)
    adjoint_field = lax.psum_scatter(adjoint_terms, "row", scatter_dimension=1, tiled=True)
    return (forward_field, adjoint_field)


def solution(mesh):
    placed = (
        P(("groups", "row"), ("col", "src")),
        P("groups", ("col", "src", "row")),
        P("groups", ("row", "col", "src")),
    )
    return jax.shard_map(
        body,
        mesh=mesh,
        in_specs=placed,
        out_specs=(P("groups", ("row", "col", "src")), P("groups", ("col", "src", "row"))),
        check_vma=False,
    )
```

profile of v0, /device:TPU:0, one launch (start us, length us, event | category | flops | bytes accessed | tf_op | source)
XLA Modules:
  0.0 75.9 jit_solution(14348635491723009299)
XLA Ops:
  7.2 0.0 copy-start
  7.2 0.0 copy-start.1
  7.2 0.0 reduce-scatter.7.cloned.1.call-start
  7.2 15.8 %all_gather.6 = bf16[8,12288]{1,0:T(8,128)(2,1)S(1)} all-gather(bf16[8,3072]{1,0:T(8,128)(2,1)} %param.4), channel_id=1, replica_groups=mesh['groups'=2,'row'=4,'col'=2,'src'=2] {'row'}, dimensions={1}, use_global_device_ids=true | all-gather | bytes 245760 | tf_op jit(solution)/shard_map/all_gather | solution.py:8
  23.0 0.0 copy-done
  23.0 1.6 %convolution_bitcast_fusion = f32[128,8]{1,0:T(8,128)} fusion(bf16[8,12288]{1,0:T(8,128)(2,1)S(1)} %all_gather.6, bf16[128,12288]{1,0:T(8,128)(2,1)S(1)} %copy-done), kind=kOutput, calls=%fused_computation | convolution fusion | flops 25165824 | bytes 3346432
  24.6 0.0 reduce-scatter.7.cloned.1.call-update
  24.6 0.0 reduce-scatter.5.cloned.1.call-start
  24.7 0.0 copy-done.1
  24.7 5.2 %all-gather = bf16[4,32,8]{1,2,0:T(8,128)(2,1)S(1)} all-gather(bf16[1,32,8]{1,2,0:T(8,128)(2,1)S(1)} %bitcast.13), channel_id=1, replica_groups=mesh['groups'=2,'row'=4,'col'=2,'src'=2] {'col','src'}, dimensions={0}, use_global_device_ids=true | all-gather | bytes 2560 | tf_op jit(solution)/shard_map/all_gather | solution.py:9
  29.9 0.1 reshape.5
  30.0 1.3 %fusion = f32[8,12288]{1,0:T(8,128)} fusion(bf16[128,8]{0,1:T(8,128)(2,1)S(1)} %reshape.5, bf16[128,12288]{1,0:T(8,128)(2,1)S(1)} %copy-done), kind=kOutput, calls=%fused_computation.1 | convolution fusion | flops 25165824 | bytes 3540992 | tf_op jit(solution)/shard_map/dot_general | solution.py:13
  31.2 0.0 reduce-scatter.5.cloned.1.call-update
  31.3 14.3 %reduce-scatter.7.cloned.1.call-done = f32[32,8]{1,0:T(8,128)} async-done(((f32[128,8]{1,0:T(8,128)}), f32[32,8]{1,0:T(8,128)}) %reduce-scatter.7.cloned.1.call-update) | async-done | bytes 1040
  45.5 1.4 %copy.8 = f32[8,32]{1,0:T(8,128)} copy(f32[8,32]{0,1:T(8,128)} %bitcast.12) | data formatting | bytes 2048
  46.9 22.2 %reduce-scatter.5.cloned.1.call-done = f32[8,3072]{1,0:T(8,128)} async-done(((f32[8,12288]{1,0:T(8,128)}), f32[8,3072]{1,0:T(8,128)}) %reduce-scatter.5.cloned.1.call-update) | async-done | bytes 98320 | tf_op jit(solution)/shard_map/reduce_scatter | solution.py:15
  (1 shorter events, 0.0 us)
Async XLA Ops:
  7.2 15.9 %copy-start = (bf16[128,12288]{1,0:T(8,128)(2,1)S(1)}, bf16[128,12288]{1,0:T(8,128)(2,1)}, u32[]{:S(2)}) copy-start(bf16[128,12288]{1,0:T(8,128)(2,1)} %param.3) | copy-start | bytes 9437188
  7.2 17.5 %copy-start.1 = (bf16[8,32]{1,0:T(8,128)(2,1)S(1)}, bf16[8,32]{1,0:T(8,128)(2,1)}, u32[]{:S(2)}) copy-start(bf16[8,32]{1,0:T(8,128)(2,1)} %param.5) | copy-start | bytes 1540
  7.2 38.3 %reduce-scatter.7.cloned.1.call-start = ((), (), s32[]{:S(2)}) async-start(), calls=%async_computation.3 | async-start | bytes 81920
  24.6 44.4 %reduce-scatter.5.cloned.1.call-start = ((), (), s32[]{:S(2)}) async-start(), calls=%async_computation.2 | async-start | bytes 491520 | tf_op jit(solution)/shard_map/reduce_scatter | solution.py:15
Sparse Core Ops, SparseCore 0:
  24.8 20.7 reduce-scatter.6
  48.5 20.5 reduce-scatter.4
where the time goes:
time: 76.2 us; the launch traced here: 75.9 us
  waiting for transfers between devices  36.5 us (48%)
  blocking collectives  21 us (28%)
  between operations  14.1 us (19%)
  matrix products  2.86 us (4%)
  local copies, waits for them, and re-layouts  1.48 us (2%)
    reduce_scatter x1, waiting for transfers between devices, body(): lax.psum_scatter(adjoint_terms, 'row', scatter_dimension=1, tiled=True)  22.2 us
    all_gather x1, blocking collectives, body(): col_block = lax.all_gather(currents, 'row', axis=1, tiled=True)  15.8 us
    unnamed x3, waiting for transfers between devices  14.3 us
    all_gather x1, blocking collectives, body(): row_block = lax.all_gather(tested, ('col', 'src'), axis=1, tiled=True)  5.16 us
    unnamed x1, matrix products  1.59 us
  transfers between devices with their start and end apart: 2, of which 2 were waited for; matrix products, arithmetic and copies ran while one was open for 4% of the time, Pallas kernels for 0%

commit v1 on v0

v1 whole, which is shorter than its diff:
```python
import functools

import jax
import jax.numpy as jnp
from jax import lax
from jax.experimental import pallas as pl
from jax.experimental.pallas import tpu as pltpu
from jax.sharding import PartitionSpec as P

MESH = pl.DeviceIdType.MESH
F32 = jnp.float32
BF16 = jnp.bfloat16


def plain(impedance, currents, tested):
    col_block = lax.all_gather(currents, "row", axis=1, tiled=True)
    row_block = lax.all_gather(tested, ("col", "src"), axis=1, tiled=True)
    forward_terms = lax.dot_general(
        col_block, impedance, (((1,), (1,)), ((), ())), preferred_element_type=F32
    )
    adjoint_terms = jnp.dot(row_block, impedance, preferred_element_type=F32)
    forward_field = lax.psum_scatter(forward_terms, ("col", "src"), scatter_dimension=1, tiled=True)
    adjoint_field = lax.psum_scatter(adjoint_terms, "row", scatter_dimension=1, tiled=True)
    return (forward_field, adjoint_field)


def kernel(
    n, nc, ns,
    imp_hbm, cur_ref, tes_ref, fwd_ref, adj_ref,
    imp, cur_all, tes_all, adj_out, adj_in, fwd_out, fwd_in,
    imp_sem, cur_send, cur_recv, tes_send, tes_recv, adj_send, adj_recv, fwd_send, fwd_recv,
):
    m = nc * ns
    s, width = cur_ref.shape
    rows = imp_hbm.shape[0]
    half = width // 2
    part = rows // m
    r = lax.axis_index("row")
    col, src = lax.axis_index("col"), lax.axis_index("src")
    q = col * ns + src

    def row_peer(k):
        return {"row": lax.rem(r + k, n)}

    def col_peer(k):
        p = lax.rem(q + k, m)
        return {"col": p // ns, "src": lax.rem(p, ns)}

    loads = []
    for k in range(n):
        first = pl.multiple_of(lax.rem(r + k, n) * width, width)
        copy = pltpu.make_async_copy(imp_hbm.at[:, pl.ds(first, width)], imp.at[k], imp_sem.at[k])
        copy.start()
        loads.append(copy)

    barrier = pltpu.get_barrier_semaphore()
    for k in range(1, n):
        pl.semaphore_signal(barrier, inc=1, device_id=row_peer(k), device_id_type=MESH)
    for k in range(1, m):
        pl.semaphore_signal(barrier, inc=1, device_id=col_peer(k), device_id_type=MESH)

    lane = lax.broadcasted_iota(jnp.int32, (s, rows), 1)
    spread = jnp.concatenate([tes_ref[...].astype(F32)] * m, axis=1)
    tes_all[0] = jnp.where(lane // part == q, spread, 0.0)
    cur = cur_ref[...].astype(F32)
    cur_all[0] = jnp.concatenate([cur[:, :half], cur[:, half:]], axis=0).astype(BF16)

    pl.semaphore_wait(barrier, n - 1 + m - 1)

    def push(ref_out, ref_in, send, recv, k, peer):
        copy = pltpu.make_async_remote_copy(
            src_ref=ref_out, dst_ref=ref_in, send_sem=send.at[k], recv_sem=recv.at[k],
            device_id=peer, device_id_type=MESH,
        )
        copy.start()
        return copy

    tes_copies = [push(tes_all.at[0], tes_all.at[m - k], tes_send, tes_recv, k, col_peer(k)) for k in range(1, m)]
    cur_copies = [push(cur_all.at[0], cur_all.at[n - k], cur_send, cur_recv, k, row_peer(k)) for k in range(1, n)]

    def forward_terms(k):
        both = cur_all[k]
        dims = (((1,), (1,)), ((), ()))
        low = lax.dot_general(both, imp[k, :, :half], dims, preferred_element_type=F32)
        high = lax.dot_general(both, imp[k, :, half:], dims, preferred_element_type=F32)
        return low[:s] + high[s:]

    for copy in tes_copies:
        copy.wait_recv()
    row_block = tes_all[0]
    for k in range(1, m):
        row_block = row_block + tes_all[k]
    row_block = row_block.astype(BF16)

    adj_copies = []
    for k in list(range(1, n)) + [0]:
        loads[k].wait()
        adj_out[k] = jnp.dot(row_block, imp[k], preferred_element_type=F32)
        if k:
            adj_copies.append(push(adj_out.at[k], adj_in.at[n - k], adj_send, adj_recv, k, row_peer(k)))

    total = forward_terms(0)
    for k in range(1, n):
        cur_copies[n - k - 1].wait_recv()
        total = total + forward_terms(k)
    fwd_out[...] = total
    fwd_copies = [push(fwd_out, fwd_in.at[m - k], fwd_send, fwd_recv, k, col_peer(k)) for k in range(1, m)]

    result = adj_out[0]
    for copy, k in zip(adj_copies, range(1, n)):
        copy.wait_recv()
        result = result + adj_in[n - k]
    adj_ref[...] = result

    for copy, k in zip(fwd_copies, range(1, m)):
        copy.wait_recv()
        total = total + fwd_in[m - k]
    mine = total[:, :part]
    for k in range(1, m):
        mine = jnp.where(q == k, total[:, k * part : (k + 1) * part], mine)
    fwd_ref[...] = mine

    for copy in tes_copies + cur_copies + adj_copies + fwd_copies:
        copy.wait_send()


def fused(n, nc, ns, impedance, currents, tested):
    m = nc * ns
    rows, _ = impedance.shape
    s, width = currents.shape
    part = rows // m
    vmem = pl.BlockSpec(memory_space=pltpu.VMEM)
    dma = pltpu.SemaphoreType.DMA
    return pl.pallas_call(
        functools.partial(kernel, n, nc, ns),
        out_shape=(
            jax.ShapeDtypeStruct((s, part), F32),
            jax.ShapeDtypeStruct((s, width), F32),
        ),
        in_specs=[pl.BlockSpec(memory_space=pl.ANY), vmem, vmem],
        out_specs=(vmem, vmem),
        scratch_shapes=[
            pltpu.VMEM((n, rows, width), BF16),
            pltpu.VMEM((n, 2 * s, width // 2), BF16),
            pltpu.VMEM((m, s, rows), F32),
            pltpu.VMEM((n, s, width), F32),
            pltpu.VMEM((n, s, width), F32),
            pltpu.VMEM((s, rows), F32),
            pltpu.VMEM((m, s, rows), F32),
            dma((n,)), dma((n,)), dma((n,)), dma((m,)), dma((m,)),
            dma((n,)), dma((n,)), dma((m,)), dma((m,)),
        ],
        compiler_params=pltpu.CompilerParams(
            collective_id=0, has_side_effects=True, vmem_limit_bytes=32 * 1024 * 1024
        ),
        cost_estimate=pl.CostEstimate(
            flops=4 * s * rows * width * n, bytes_accessed=2 * rows * width * n, transcendentals=0
        ),
    )(impedance, currents, tested)


def solution(mesh):
    n, nc, ns = mesh.shape["row"], mesh.shape["col"], mesh.shape["src"]

    def body(impedance, currents, tested):
        s, width = currents.shape
        rows = impedance.shape[0]
        if s == 8 and width % 256 == 0 and rows % 128 == 0:
            return fused(n, nc, ns, impedance, currents, tested)
        return plain(impedance, currents, tested)

    placed = (
        P(("groups", "row"), ("col", "src")),
        P("groups", ("col", "src", "row")),
        P("groups", ("row", "col", "src")),
    )
    return jax.shard_map(
        body,
        mesh=mesh,
        in_specs=placed,
        out_specs=(P("groups", ("row", "col", "src")), P("groups", ("col", "src", "row"))),
        check_vma=False,
    )
```

time: 76.2 us -> 24 us (0.31)
  waiting for transfers between devices: 36.5 us -> 0 us
  blocking collectives: 21 us -> 0 us
  Pallas kernels: 0 us -> 18.5 us
  between operations: 14.1 us -> 0.65 us
  local copies, waits for them, and re-layouts: 1.48 us -> 4.6 us
  matrix products: 2.86 us -> 0 us
    reduce_scatter x1 -> x0, waiting for transfers between devices: 22.2 us -> none  [body(): lax.psum_scatter(adjoint_terms, 'row', scatter_dimension=1, tiled=True)]
    all_gather x2 -> x0, blocking collectives: 21 us -> none  [the longest x1 15.8 us: body(): col_block = lax.all_gather(currents, 'row', axis=1, tiled=True)]
    pallas_call x0 -> x1, Pallas kernels: none -> 18.5 us  [fused(): pl.pallas_call(functools.partial(kernel, n, nc, ns), out_shape=(jax.Shape...]
    unnamed x3 -> x0, waiting for transfers between devices: 14.3 us -> none
    unnamed x6 -> x8, local copies, waits for them, and re-layouts: 1.48 us -> 4.6 us
    unnamed x1 -> x0, matrix products: 1.59 us -> none
    dot_general x1 -> x0, matrix products: 1.28 us -> none  [body(): jnp.dot(row_block, impedance, preferred_element_type=jnp.float32)]
  transfers between devices with their start and end apart: 2 -> 0, of which waited for: 2 -> 0; matrix products, arithmetic and copies ran while one was open for 4% -> 0% of each run, Pallas kernels for 0% -> 0%
where the time goes in v1:
time: 24 us; the launch traced here: 23.8 us
  Pallas kernels  18.5 us (77%)
  local copies, waits for them, and re-layouts  4.6 us (19%)
  between operations  0.65 us (3%)
    pallas_call x1, Pallas kernels, fused(): pl.pallas_call(functools.partial(kernel, n, nc, ns), out_shape=(jax.Shape...  18.5 us
    unnamed x8, local copies, waits for them, and re-layouts  4.6 us

profile of v1, /device:TPU:0, one launch (start us, length us, event | category | flops | bytes accessed | tf_op | source)
XLA Modules:
  0.0 23.8 jit_solution(12774042730554510710)
XLA Ops:
  0.6 0.0 copy-start
  0.6 1.9 %copy-done = bf16[128,12288]{1,0:T(8,128)(2,1)S(1)} copy-done((bf16[128,12288]{1,0:T(8,128)(2,1)S(1)}, bf16[128,12288]{1,0:T(8,128)(2,1)}, u32[]{:S(2)}) %copy-start) | copy-done | bytes 3145752
  2.5 0.0 copy-start.1
  2.5 0.8 %copy-done.1 = bf16[8,3072]{1,0:T(8,128)(2,1)S(1)} copy-done((bf16[8,3072]{1,0:T(8,128)(2,1)S(1)}, bf16[8,3072]{1,0:T(8,128)(2,1)}, u32[]{:S(2)}) %copy-start.1) | copy-done | bytes 49176
  3.3 0.0 copy-start.2
  3.3 0.7 %copy-done.2 = bf16[8,32]{1,0:T(8,128)(2,1)S(1)} copy-done((bf16[8,32]{1,0:T(8,128)(2,1)S(1)}, bf16[8,32]{1,0:T(8,128)(2,1)}, u32[]{:S(2)}) %copy-start.2) | copy-done | bytes 536
  4.0 18.5 %shard_map.50 = (f32[8,32]{1,0:T(8,128)S(1)}, f32[8,3072]{1,0:T(8,128)S(1)}) custom-call(bf16[128,12288]{1,0:T(8,128)(2,1)S(1)} %copy-done, bf16[8,3072]{1,0:T(8,128)(2,1)S(1)} %copy-done.1, bf16[8,32]{1,0:T(8,128)(2,1)S(1)} %copy-done.2), custom_call_target="tpu_custom_call" | custom-call | flops 50331648 | bytes 3145728 | tf_op jit(solution)/shard_map/pallas_call | solution.py:134
  22.5 0.6 %copy.7 = f32[8,32]{1,0:T(8,128)} copy(f32[8,32]{1,0:T(8,128)S(1)} %get-tuple-element.4) | data formatting | bytes 2048
  23.1 0.6 %copy.8 = f32[8,3072]{1,0:T(8,128)} copy(f32[8,3072]{1,0:T(8,128)S(1)} %get-tuple-element.5) | data formatting | bytes 196608
Async XLA Ops:
  0.6 1.9 %copy-start = (bf16[128,12288]{1,0:T(8,128)(2,1)S(1)}, bf16[128,12288]{1,0:T(8,128)(2,1)}, u32[]{:S(2)}) copy-start(bf16[128,12288]{1,0:T(8,128)(2,1)} %imp_hbm.1) | copy-start | bytes 9437188
  2.5 0.8 %copy-start.1 = (bf16[8,3072]{1,0:T(8,128)(2,1)S(1)}, bf16[8,3072]{1,0:T(8,128)(2,1)}, u32[]{:S(2)}) copy-start(bf16[8,3072]{1,0:T(8,128)(2,1)} %cur_ref.1) | copy-start | bytes 147460
  3.3 0.7 %copy-start.2 = (bf16[8,32]{1,0:T(8,128)(2,1)S(1)}, bf16[8,32]{1,0:T(8,128)(2,1)}, u32[]{:S(2)}) copy-start(bf16[8,32]{1,0:T(8,128)(2,1)} %tes_ref.1) | copy-start | bytes 1540

commit v2 on v1

v2 whole, which is shorter than its diff:
```python
import functools

import jax
import jax.numpy as jnp
from jax import lax
from jax.experimental import pallas as pl
from jax.experimental.pallas import tpu as pltpu
from jax.sharding import PartitionSpec as P

MESH = pl.DeviceIdType.MESH
F32 = jnp.float32
BF16 = jnp.bfloat16
SPAN = 2.0**14


def plain(impedance, currents, tested):
    col_block = lax.all_gather(currents, "row", axis=1, tiled=True)
    row_block = lax.all_gather(tested, ("col", "src"), axis=1, tiled=True)
    forward_terms = lax.dot_general(
        col_block, impedance, (((1,), (1,)), ((), ())), preferred_element_type=F32
    )
    adjoint_terms = jnp.dot(row_block, impedance, preferred_element_type=F32)
    forward_field = lax.psum_scatter(forward_terms, ("col", "src"), scatter_dimension=1, tiled=True)
    adjoint_field = lax.psum_scatter(adjoint_terms, "row", scatter_dimension=1, tiled=True)
    return (forward_field, adjoint_field)


def encode(block):
    s, width = block.shape
    half = width // 2
    top = jnp.max(jnp.abs(block), axis=1, keepdims=True).astype(BF16).astype(F32)
    scale = jnp.where(top > 0.0, 1.0 / top, 0.0)
    unit = block * scale * SPAN
    square = unit * unit
    fourth = square * square
    eighth = fourth * fourth
    coded = jnp.where(unit < 0.0, -eighth, eighth)
    tops = jnp.broadcast_to(top, (s, 128))
    low = jnp.concatenate([coded[:, :half], tops], axis=1)
    high = jnp.concatenate([coded[:, half:], tops], axis=1)
    return jnp.concatenate([low, high], axis=0).astype(BF16)


def decode(wire):
    both, cols = wire.shape
    s, half = both // 2, cols - 128
    coded = wire.astype(F32)
    coded = jnp.concatenate([coded[:s, :half], coded[s:, :half]], axis=1)
    top = wire.astype(F32)[:s, half : half + 1] * (1.0 / SPAN)
    size = jnp.abs(coded)
    fourth_root = lax.rsqrt(lax.rsqrt(size))
    root = fourth_root * lax.rsqrt(fourth_root)
    root = jnp.where(size > 0.0, root, 0.0) * top
    return jnp.where(coded < 0.0, -root, root)


def kernel(
    n, nc, ns,
    imp_hbm, cur_hbm, tes_hbm, fwd_ref, adj_ref,
    imp, cur_ref, cur_all, tes_all, adj_out, adj_in, fwd_out, fwd_in,
    in_sem, imp_sem, cur_send, cur_recv, tes_send, tes_recv, adj_send, adj_recv, fwd_send, fwd_recv,
):
    m = nc * ns
    s, width = cur_hbm.shape
    rows = imp_hbm.shape[0]
    part = rows // m
    r = lax.axis_index("row")
    q = lax.axis_index("col") * ns + lax.axis_index("src")

    def row_at(k):
        return lax.rem(r + k, n)

    def row_peer(k):
        return {"row": row_at(k)}

    def col_peer(k):
        p = lax.rem(q + k, m)
        return {"col": p // ns, "src": lax.rem(p, ns)}

    tes_load = pltpu.make_async_copy(tes_hbm, tes_all.at[q], in_sem.at[0])
    tes_load.start()
    cur_load = pltpu.make_async_copy(cur_hbm, cur_ref, in_sem.at[1])
    cur_load.start()
    loads = []
    for k in range(n):
        first = pl.multiple_of(row_at(k) * width, width)
        copy = pltpu.make_async_copy(imp_hbm.at[:, pl.ds(first, width)], imp.at[k], imp_sem.at[k])
        copy.start()
        loads.append(copy)

    barrier = pltpu.get_barrier_semaphore()
    for k in range(1, m):
        pl.semaphore_signal(barrier, inc=1, device_id=col_peer(k), device_id_type=MESH)
    for k in range(1, n):
        pl.semaphore_signal(barrier, inc=1, device_id=row_peer(k), device_id_type=MESH)

    cur_load.wait()
    half = width // 2
    cur = cur_ref[...].astype(F32)
    cur_all[0] = jnp.concatenate([cur[:, :half], cur[:, half:]], axis=0).astype(BF16)
    tes_load.wait()
    pl.semaphore_wait(barrier, n - 1 + m - 1)

    def push(ref_out, ref_in, send, recv, k, peer):
        copy = pltpu.make_async_remote_copy(
            src_ref=ref_out, dst_ref=ref_in, send_sem=send.at[k], recv_sem=recv.at[k],
            device_id=peer, device_id_type=MESH,
        )
        copy.start()
        return copy

    away = list(range(1, n))
    tes_copies = [push(tes_all.at[q], tes_all.at[q], tes_send, tes_recv, k, col_peer(k)) for k in range(1, m)]
    cur_copies = [push(cur_all.at[0], cur_all.at[n - k], cur_send, cur_recv, k, row_peer(k)) for k in away]

    def forward_terms(k):
        both = cur_all[k]
        dims = (((1,), (1,)), ((), ()))
        low = lax.dot_general(both, imp[k, :, :half], dims, preferred_element_type=F32)
        high = lax.dot_general(both, imp[k, :, half:], dims, preferred_element_type=F32)
        return low[:s] + high[s:]

    for copy in tes_copies:
        copy.wait_recv()
    row_block = jnp.concatenate([tes_all[p].astype(F32) for p in range(m)], axis=1).astype(BF16)

    adj_copies = []
    for k in away:
        loads[k].wait()
        adj_out[k] = encode(jnp.dot(row_block, imp[k], preferred_element_type=F32))
        adj_copies.append(push(adj_out.at[k], adj_in.at[n - k], adj_send, adj_recv, k, row_peer(k)))

    loads[0].wait()
    total = forward_terms(0)
    for copy, k in zip(cur_copies, away):
        copy.wait_recv()
        total = total + forward_terms(n - k)
    fwd_out[...] = total
    fwd_copies = [push(fwd_out, fwd_in.at[m - k], fwd_send, fwd_recv, k, col_peer(k)) for k in range(1, m)]

    result = jnp.dot(row_block, imp[0], preferred_element_type=F32)
    for copy, k in zip(reversed(adj_copies), reversed(away)):
        copy.wait_recv()
        result = result + decode(adj_in[n - k])
    adj_ref[...] = result

    for copy, k in zip(fwd_copies, range(1, m)):
        copy.wait_recv()
        total = total + fwd_in[m - k]
    mine = total[:, :part]
    for k in range(1, m):
        mine = jnp.where(q == k, total[:, k * part : (k + 1) * part], mine)
    fwd_ref[...] = mine

    for copy in tes_copies + cur_copies + adj_copies + fwd_copies:
        copy.wait_send()


def fused(n, nc, ns, impedance, currents, tested):
    m = nc * ns
    rows, _ = impedance.shape
    s, width = currents.shape
    part = rows // m
    vmem = pl.BlockSpec(memory_space=pltpu.VMEM)
    dma = pltpu.SemaphoreType.DMA
    return pl.pallas_call(
        functools.partial(kernel, n, nc, ns),
        out_shape=(pltpu.VMEM((s, part), F32), pltpu.VMEM((s, width), F32)),
        in_specs=[pl.BlockSpec(memory_space=pltpu.HBM)] * 3,
        out_specs=(vmem, vmem),
        scratch_shapes=[
            pltpu.VMEM((n, rows, width), BF16),
            pltpu.VMEM((s, width), BF16),
            pltpu.VMEM((n, 2 * s, width // 2), BF16),
            pltpu.VMEM((m, s, part), BF16),
            pltpu.VMEM((n, 2 * s, width // 2 + 128), BF16),
            pltpu.VMEM((n, 2 * s, width // 2 + 128), BF16),
            pltpu.VMEM((s, rows), F32),
            pltpu.VMEM((m, s, rows), F32),
            dma((2,)), dma((n,)), dma((n,)), dma((n,)), dma((m,)), dma((m,)),
            dma((n,)), dma((n,)), dma((m,)), dma((m,)),
        ],
        compiler_params=pltpu.CompilerParams(
            collective_id=0, has_side_effects=True, vmem_limit_bytes=32 * 1024 * 1024
        ),
        cost_estimate=pl.CostEstimate(
            flops=4 * s * rows * width * n, bytes_accessed=2 * rows * width * n, transcendentals=0
        ),
    )(*[pltpu.with_memory_space_constraint(x, pltpu.HBM) for x in (impedance, currents, tested)])


def solution(mesh):
    n, nc, ns = mesh.shape["row"], mesh.shape["col"], mesh.shape["src"]

    def body(impedance, currents, tested):
        s, width = currents.shape
        rows = impedance.shape[0]
        if s == 8 and n & (n - 1) == 0 and width % 256 == 0 and rows % 128 == 0:
            return fused(n, nc, ns, impedance, currents, tested)
        return plain(impedance, currents, tested)

    placed = (
        P(("groups", "row"), ("col", "src")),
        P("groups", ("col", "src", "row")),
        P("groups", ("row", "col", "src")),
    )
    return jax.shard_map(
        body,
        mesh=mesh,
        in_specs=placed,
        out_specs=(P("groups", ("row", "col", "src")), P("groups", ("col", "src", "row"))),
        check_vma=False,
    )
```

time: 24 us -> 17.3 us (0.72)
  local copies, waits for them, and re-layouts: 4.6 us -> 1.24 us
  Pallas kernels: 18.5 us -> 15.3 us
    unnamed x8 -> x2, local copies, waits for them, and re-layouts: 4.6 us -> 1.24 us
    pallas_call x1, Pallas kernels: 18.5 us -> 15.3 us  [fused(): pl.pallas_call(functools.partial(kernel, n, nc, ns), out_shape=(pltpu.VME...]
where the time goes in v2:
time: 17.3 us; the launch traced here: 17.2 us
  Pallas kernels  15.3 us (88%)
  local copies, waits for them, and re-layouts  1.24 us (7%)
  between operations  0.64 us (4%)
    pallas_call x1, Pallas kernels, fused(): pl.pallas_call(functools.partial(kernel, n, nc, ns), out_shape=(pltpu.VME...  15.3 us
    unnamed x2, local copies, waits for them, and re-layouts  1.24 us

profile of v2, /device:TPU:0, one launch (start us, length us, event | category | flops | bytes accessed | tf_op | source)
XLA Modules:
  0.0 17.2 jit_solution(6761512177436583588)
XLA Ops:
  0.6 15.3 %shard_map.50 = (f32[8,32]{1,0:T(8,128)S(1)}, f32[8,3072]{1,0:T(8,128)S(1)}) custom-call(bf16[128,12288]{1,0:T(8,128)(2,1)} %imp_hbm.1, bf16[8,3072]{1,0:T(8,128)(2,1)} %cur_hbm.1, bf16[8,32]{1,0:T(8,128)(2,1)} %tes_hbm.1), custom_call_target="tpu_custom_call" | custom-call | flops 50331648 | bytes 3145728 | tf_op jit(solution)/shard_map/pallas_call | solution.py:166
  15.9 0.6 %copy.7 = f32[8,32]{1,0:T(8,128)} copy(f32[8,32]{1,0:T(8,128)S(1)} %get-tuple-element.2) | data formatting | bytes 2048
  16.5 0.6 %copy.8 = f32[8,3072]{1,0:T(8,128)} copy(f32[8,3072]{1,0:T(8,128)S(1)} %get-tuple-element.3) | data formatting | bytes 196608

commit v3 on v2

--- a/solution.py
+++ b/solution.py
@@ -81,18 +81,18 @@
     tes_load.start()
     cur_load = pltpu.make_async_copy(cur_hbm, cur_ref, in_sem.at[1])
     cur_load.start()
+    barrier = pltpu.get_barrier_semaphore()
+    for k in range(1, m):
+        pl.semaphore_signal(barrier, inc=1, device_id=col_peer(k), device_id_type=MESH)
+    for k in range(1, n):
+        pl.semaphore_signal(barrier, inc=1, device_id=row_peer(k), device_id_type=MESH)
+
     loads = []
     for k in range(n):
         first = pl.multiple_of(row_at(k) * width, width)
         copy = pltpu.make_async_copy(imp_hbm.at[:, pl.ds(first, width)], imp.at[k], imp_sem.at[k])
         copy.start()
         loads.append(copy)
-
-    barrier = pltpu.get_barrier_semaphore()
-    for k in range(1, m):
-        pl.semaphore_signal(barrier, inc=1, device_id=col_peer(k), device_id_type=MESH)
-    for k in range(1, n):
-        pl.semaphore_signal(barrier, inc=1, device_id=row_peer(k), device_id_type=MESH)
 
     cur_load.wait()
     half = width // 2
@@ -139,7 +139,7 @@
     fwd_copies = [push(fwd_out, fwd_in.at[m - k], fwd_send, fwd_recv, k, col_peer(k)) for k in range(1, m)]
 
     result = jnp.dot(row_block, imp[0], preferred_element_type=F32)
-    for copy, k in zip(reversed(adj_copies), reversed(away)):
+    for copy, k in zip(adj_copies, away):
         copy.wait_recv()
         result = result + decode(adj_in[n - k])
     adj_ref[...] = result
@@ -154,6 +154,15 @@
 
     for copy in tes_copies + cur_copies + adj_copies + fwd_copies:
         copy.wait_send()
+
+
+def deliver(fwd_ref, adj_ref, fwd_hbm, adj_hbm, sem):
+    adj_copy = pltpu.make_async_copy(adj_ref, adj_hbm, sem.at[0])
+    fwd_copy = pltpu.make_async_copy(fwd_ref, fwd_hbm, sem.at[1])
+    adj_copy.start()
+    fwd_copy.start()
+    adj_copy.wait()
+    fwd_copy.wait()
 
 
 def fused(n, nc, ns, impedance, currents, tested):
@@ -163,7 +172,7 @@
     part = rows // m
     vmem = pl.BlockSpec(memory_space=pltpu.VMEM)
     dma = pltpu.SemaphoreType.DMA
-    return pl.pallas_call(
+    fields = pl.pallas_call(
         functools.partial(kernel, n, nc, ns),
         out_shape=(pltpu.VMEM((s, part), F32), pltpu.VMEM((s, width), F32)),
         in_specs=[pl.BlockSpec(memory_space=pltpu.HBM)] * 3,
@@ -187,6 +196,13 @@
             flops=4 * s * rows * width * n, bytes_accessed=2 * rows * width * n, transcendentals=0
         ),
     )(*[pltpu.with_memory_space_constraint(x, pltpu.HBM) for x in (impedance, currents, tested)])
+    return pl.pallas_call(
+        deliver,
+        out_shape=(pltpu.HBM((s, part), F32), pltpu.HBM((s, width), F32)),
+        in_specs=[vmem, vmem],
+        out_specs=(pl.BlockSpec(memory_space=pltpu.HBM), pl.BlockSpec(memory_space=pltpu.HBM)),
+        scratch_shapes=[dma((2,))],
+    )(*[pltpu.with_memory_space_constraint(x, pltpu.VMEM) for x in fields])
 
 
 def solution(mesh):

time: 17.3 us -> 16.8 us (0.971)
  local copies, waits for them, and re-layouts: 1.24 us -> 0 us
  Pallas kernels: 15.3 us -> 16 us
    unnamed x2 -> x0, local copies, waits for them, and re-layouts: 1.24 us -> none
    pallas_call x0 -> x1, Pallas kernels: none -> 0.66 us  [fused(): pl.pallas_call(deliver, out_shape=(pltpu.HBM((s, part), F32), pltpu.HBM((...]
where the time goes in v3:
time: 16.8 us; the launch traced here: 16.6 us
  Pallas kernels  16 us (95%)
  between operations  0.64 us (4%)
    pallas_call x1, Pallas kernels, fused(): pl.pallas_call(functools.partial(kernel, n, nc, ns), out_shape=(pltpu.VME...  15.3 us
    pallas_call x1, Pallas kernels, fused(): pl.pallas_call(deliver, out_shape=(pltpu.HBM((s, part), F32), pltpu.HBM((...  0.66 us

profile of v3, /device:TPU:0, one launch (start us, length us, event | category | flops | bytes accessed | tf_op | source)
XLA Modules:
  0.0 16.6 jit_solution(14121482941840085871)
XLA Ops:
  0.6 15.3 %shard_map.50 = (f32[8,32]{1,0:T(8,128)S(1)}, f32[8,3072]{1,0:T(8,128)S(1)}) custom-call(bf16[128,12288]{1,0:T(8,128)(2,1)} %imp_hbm.1, bf16[8,3072]{1,0:T(8,128)(2,1)} %cur_hbm.1, bf16[8,32]{1,0:T(8,128)(2,1)} %tes_hbm.1), custom_call_target="tpu_custom_call" | custom-call | flops 50331648 | bytes 3145728 | tf_op jit(solution)/shard_map/pallas_call | solution.py:175
  16.0 0.7 %shard_map.51 = (f32[8,32]{1,0:T(8,128)}, f32[8,3072]{1,0:T(8,128)}) custom-call(f32[8,32]{1,0:T(8,128)S(1)} %get-tuple-element.4.fwd_ref, f32[8,3072]{1,0:T(8,128)S(1)} %get-tuple-element.5.adj_ref), custom_call_target="tpu_custom_call" | custom-call | tf_op jit(solution)/shard_map/pallas_call | solution.py:199

commit v4 on v3

--- a/solution.py
+++ b/solution.py
@@ -87,12 +87,12 @@
     for k in range(1, n):
         pl.semaphore_signal(barrier, inc=1, device_id=row_peer(k), device_id_type=MESH)
 
-    loads = []
-    for k in range(n):
+    loads = [None] * n
+    for k in list(range(1, n)) + [0]:
         first = pl.multiple_of(row_at(k) * width, width)
         copy = pltpu.make_async_copy(imp_hbm.at[:, pl.ds(first, width)], imp.at[k], imp_sem.at[k])
         copy.start()
-        loads.append(copy)
+        loads[k] = copy
 
     cur_load.wait()
     half = width // 2

time: 16.8 us -> 16.8 us (level)
  no operation moved by 1% of the time
where the time goes in v4:
time: 16.8 us; the launch traced here: 16.6 us
  Pallas kernels  16 us (95%)
  between operations  0.64 us (4%)
    pallas_call x1, Pallas kernels, fused(): pl.pallas_call(functools.partial(kernel, n, nc, ns), out_shape=(pltpu.VME...  15.3 us
    pallas_call x1, Pallas kernels, fused(): pl.pallas_call(deliver, out_shape=(pltpu.HBM((s, part), F32), pltpu.HBM((...  0.66 us

profile of v4, /device:TPU:0, one launch (start us, length us, event | category | flops | bytes accessed | tf_op | source)
XLA Modules:
  0.0 16.6 jit_solution(16952509419015277176)
XLA Ops:
  0.6 15.3 %shard_map.50 = (f32[8,32]{1,0:T(8,128)S(1)}, f32[8,3072]{1,0:T(8,128)S(1)}) custom-call(bf16[128,12288]{1,0:T(8,128)(2,1)} %imp_hbm.1, bf16[8,3072]{1,0:T(8,128)(2,1)} %cur_hbm.1, bf16[8,32]{1,0:T(8,128)(2,1)} %tes_hbm.1), custom_call_target="tpu_custom_call" | custom-call | flops 50331648 | bytes 3145728 | tf_op jit(solution)/shard_map/pallas_call | solution.py:175
  15.9 0.7 %shard_map.51 = (f32[8,32]{1,0:T(8,128)}, f32[8,3072]{1,0:T(8,128)}) custom-call(f32[8,32]{1,0:T(8,128)S(1)} %get-tuple-element.4.fwd_ref, f32[8,3072]{1,0:T(8,128)S(1)} %get-tuple-element.5.adj_ref), custom_call_target="tpu_custom_call" | custom-call | tf_op jit(solution)/shard_map/pallas_call | solution.py:199
